TPU v7x, 1024 devices: a whole 4x4x32 slice. The times are simulated.
1024 devices in a mesh: dp: 128 (over z_lo, y, core), tensor: 8 (over z_hi, x).
Axes of the slice: x: 4, y: 4, z: 32 (z_hi: 2, z_lo: 16; z = z_hi * 16 + z_lo), core: 2. Of those that a mesh axis runs over, the one named last changes fastest.
Arguments:
- grads: bfloat16 [128, 4096, 1024], P('dp', None, 'tensor'), may hold values from -16 to 16
- errors: bfloat16 [128, 4096, 1024], P('dp', None, 'tensor'), may hold values from -3 to 3
- basis: float32 [1024, 64], P('tensor'), may hold values from -6 to 6
Outputs:
- approx: bfloat16 [4096, 1024], P(None, 'tensor')
- new_errors: bfloat16 [128, 4096, 1024], P('dp', None, 'tensor')
- new_basis: float32 [1024, 64], P('tensor')
All inputs are finite; a program needn't handle non-finite values.
Results may differ from a plain program's by a relative error of at most 0.009.
Values may be sent and summed in bfloat16 or wider, within the bound.
A program may use at most 32 MiB of HBM per device.

v0:
```python
import jax
import jax.numpy as jnp
from jax import lax
from jax.sharding import PartitionSpec as P


def orthonormalize(left_rows, gram_matrix):
    lower_factor = jnp.linalg.cholesky(gram_matrix)
    return lax.linalg.triangular_solve(
        lower_factor, left_rows, left_side=False, lower=True, transpose_a=True
    ).astype(jnp.bfloat16)


def local(grads, errors, basis):
    replicas = lax.axis_size("dp")
    combined = (grads[0].astype(jnp.float32) + errors[0].astype(jnp.float32)).astype(jnp.bfloat16)
    left_part = jnp.dot(combined, basis.astype(jnp.bfloat16), preferred_element_type=jnp.float32)
    left_factor = lax.psum(left_part, ("dp", "tensor")) / replicas
    gram_matrix = jnp.dot(left_factor.T, left_factor, precision=lax.Precision.HIGHEST)
    orthonormal = orthonormalize(left_factor, gram_matrix)
    right_part = lax.dot_general(
        combined, orthonormal, (((0,), (0,)), ((), ())), preferred_element_type=jnp.float32
    )
    new_basis = lax.psum(right_part, "dp") / replicas
    basis_new_bf = new_basis.astype(jnp.bfloat16)
    full_approx = lax.dot_general(
        orthonormal, basis_new_bf, (((1,), (1,)), ((), ())), preferred_element_type=jnp.float32
    )
    new_errors = (combined.astype(jnp.float32) - full_approx).astype(jnp.bfloat16)[None]
    return (full_approx.astype(jnp.bfloat16), new_errors, new_basis)


def solution(mesh):
    placed = (P("dp", None, "tensor"), P("dp", None, "tensor"), P("tensor", None))
    return jax.shard_map(
        local,
        mesh=mesh,
        in_specs=placed,
        out_specs=(P(None, "tensor"), P("dp", None, "tensor"), P("tensor", None)),
        check_vma=False,
    )
```

profile of v0, /device:TPU:1, one launch (start us, length us, event | category | flops | bytes accessed | tf_op | source)
XLA Modules:
  0.0 2386.3 jit_solution(7872622361316460316)
XLA Ops:
  7.2 0.0 all-reduce.2.cloned.1.call-start
  7.2 3.0 fusion.12
  10.2 0.0 all-reduce.2.cloned.1.call-update
  10.2 903.6 %all-reduce.2.cloned.1.call-done = f32[4096,64]{0,1:T(8,128)} async-done(((f32[4096,64]{0,1:T(8,128)}), f32[4096,64]{0,1:T(8,128)}) %all-reduce.2.cloned.1.call-update) | async-done | bytes 1048592 | tf_op jit(solution)/shard_map/psum | solution.py:18
  913.8 0.0 copy-start.1
  913.8 2.7 fusion.3
  916.5 0.0 copy-start
  916.5 0.1 copy.6
  916.6 5.8 cholesky.16
  922.4 0.6 compare_reduce_fusion
  923.1 0.7 fusion.7
  923.8 4.9 custom-call.6
  928.6 2.3 convolution_convert_fusion
  931.0 0.0 copy-done.1
  931.0 0.0 copy-done
  931.0 0.4 fusion.16
  931.4 1446.1 %psum.15 = f32[128,64]{0,1:T(8,128)S(1)} all-reduce(f32[128,64]{0,1:T(8,128)S(1)} %fusion.16), channel_id=1, replica_groups=mesh['dp'=128,'tensor'=8] {'dp'}, use_global_device_ids=true, to_apply=%region_3.4 | all-reduce | flops 8192 | bytes 65536 | tf_op jit(solution)/shard_map/psum | solution.py:24
  2377.5 0.0 copy-start.2
  2377.5 2.0 fusion.1
  2379.5 0.0 copy-done.2
  (3 shorter events, 0.0 us)
Async XLA Ops:
  7.2 906.6 %all-reduce.2.cloned.1.call-start = ((), (), s32[]{:S(2)}) async-start(), calls=%async_computation | async-start | bytes 2097152 | tf_op jit(solution)/shard_map/psum | solution.py:18
  913.8 17.2 copy-start.1
  916.5 14.5 copy-start
  2377.5 2.0 copy-start.2
Sparse Core Ops, SparseCore 0:
  14.0 899.7 all-reduce.1
where the time goes:
time: 2410 us; the launch traced here: 2390 us
  blocking collectives  1450 us (60%)
  waiting for transfers between devices  904 us (38%)
    psum x1, blocking collectives, local(): new_basis = lax.psum(right_part, 'dp') / replicas  1450 us
    psum x1, waiting for transfers between devices, local(): left_factor = lax.psum(left_part, ('dp', 'tensor')) / replicas  904 us
  transfers between devices with their start and end apart: 1, of which 1 were waited for; matrix products, arithmetic and copies ran while one was open for 0% of the time, Pallas kernels for 0%

commit v1 on v0

v1 whole, which is shorter than its diff:
```python
import functools

import jax
import jax.numpy as jnp
from jax import lax
from jax.experimental import pallas as pl
from jax.experimental.pallas import tpu as pltpu
from jax.sharding import PartitionSpec as P

MESH = pl.DeviceIdType.MESH
F32, BF16 = jnp.float32, jnp.bfloat16
COLS, RANK = 128, 64
HALF = 2048
OWN = 1024
BLOCK = 64
PART = 16
CHUNK = 256


def device(x, y, z, core):
    return ((z & 15) * 8 + y * 2 + core, (z >> 4) * 4 + x)


def rows(start, size):
    return pl.ds(pl.multiple_of(start, size), size)


def send(src, dst, send_sem, recv_sem, to):
    copy = pltpu.make_async_remote_copy(
        src_ref=src, dst_ref=dst, send_sem=send_sem, recv_sem=recv_sem, device_id=to, device_id_type=MESH
    )
    copy.start()


def wait(ref, sem):
    pltpu.make_async_copy(ref, ref, sem).wait()


def split(value):
    high = value.astype(BF16)
    low = (value - high.astype(F32)).astype(BF16)
    return high, low


def twice(value):
    zeros = jnp.zeros_like(value)
    return jnp.concatenate(
        [jnp.concatenate([value, zeros], axis=1), jnp.concatenate([zeros, value], axis=1)], axis=0
    )


def inverse_factor(gram):
    tiles = RANK // 8
    rows_at = lax.broadcasted_iota(jnp.int32, (8, 128), 0)
    m = [gram[8 * b : 8 * b + 8, :] for b in range(tiles)]
    pivots = []
    for k in range(RANK):
        at, sub = divmod(k, 8)
        pivot_row = m[at][sub : sub + 1, :]
        pivot = pivot_row[:, k : k + 1]
        pivots.append(pivot)
        scaled = pivot_row * (1.0 / pivot)
        for b in range(at, tiles):
            update = m[b][:, k : k + 1] * scaled
            if b == at:
                update = jnp.where(rows_at > sub, update, 0.0)
            m[b] = m[b] - update
    out = []
    for b in range(tiles):
        scale = jnp.concatenate(pivots[8 * b : 8 * b + 8], axis=0)
        out.append(m[b] * lax.rsqrt(scale))
    return jnp.concatenate(out, axis=0)


def exchange_kernel(
    replicas, grads, errors, basis, q_out, comb_out, right_out,
    g_in, e_in, comb, blocks, part, from_core, plane_in, plane_sum, near_in, near_sum, far_in, full, pieces, grams, q,
    right, right_core, right_y, right_near, right_near_sum, right_far, right_full,
    local_sem, core_send, core_recv, send_sem, recv_sem, far_send, far_recv,
):
    d, t = lax.axis_index("dp"), lax.axis_index("tensor")
    core, y, z, x = d & 1, (d >> 1) & 3, (t >> 2) * 16 + (d >> 3), t & 3
    near, far, mine = z & 3, z >> 2, y * 4 + x
    other = device(x, y, z, 1 - core)
    own, theirs = core * OWN, (1 - core) * OWN

    def plane(i, j):
        return (x + j) & 3, (y + i) & 3

    def near_at(o):
        return (near + o) & 3

    def near_device(o):
        return device(x, y, (z & 28) | near_at(o), core)

    def in_line(o):
        return device(x, y, (z & 19) | (((far + o) & 3) << 2), core)

    up, down = device(x, y, (z + 4) & 31, core), device(x, y, (z + 28) & 31, core)
    offsets = [(i, j) for i in range(4) for j in range(4) if (i, j) != (0, 0)]

    for n, start in enumerate((theirs, own)):
        for base in (0, HALF):
            here = rows(base + start, OWN)
            pltpu.make_async_copy(grads.at[0, here], g_in.at[here], local_sem.at[n]).start()
            pltpu.make_async_copy(errors.at[0, here], e_in.at[here], local_sem.at[n]).start()

    barrier = pltpu.get_barrier_semaphore()
    partners = [other, up, down] + [near_device(o) for o in (1, 2, 3)]
    partners += [device(*plane(i, j), z, core) for i, j in offsets]
    for to in partners:
        pl.semaphore_signal(barrier, inc=1, device_id=to, device_id_type=MESH)

    blocks[...] = twice(basis[...].astype(BF16))
    lanes = lax.broadcasted_iota(jnp.int32, (RANK, 128), 1)
    at = lax.broadcasted_iota(jnp.int32, (RANK, 128), 0)

    def product(start):
        both = []
        for base in (0, HALF):
            here = rows(base + start, CHUNK)
            both.append((g_in[here, :].astype(F32) + e_in[here, :].astype(F32)).astype(BF16))
        value = jnp.concatenate(both, axis=1)
        comb[rows(start, CHUNK), :] = value
        part[rows(start, CHUNK), :] = lax.dot_general(
            value, blocks[...], (((1,), (1,)), ((), ())), preferred_element_type=F32
        )

    order = [((y + i) & 3) * CHUNK for i in range(4)]
    wait(g_in, local_sem.at[0])
    for i in range(4):
        product(theirs + order[i])
    pl.semaphore_wait(barrier, len(partners))
    for i in range(4):
        send(part.at[rows(theirs + order[i], CHUNK)], from_core.at[i], core_send.at[i], core_recv.at[i], other)
    wait(g_in, local_sem.at[1])
    for i in range(4):
        product(own + order[i])
    for i in range(4):
        wait(from_core.at[i], core_recv.at[i])
        here = rows(own + order[i], CHUNK)
        part[here, :] = part[here, :] + from_core[i]
        for j in range(4):
            if (i, j) != (0, 0):
                px, py = plane(i, j)
                src = part.at[rows(own + (py * 4 + px) * BLOCK, BLOCK)]
                send(src, plane_in.at[mine], send_sem.at[0], recv_sem.at[0], device(px, py, z, core))
    comb_copy = pltpu.make_async_copy(comb, comb_out, local_sem.at[2])
    comb_copy.start()
    plane_in[mine] = part[rows(own + mine * BLOCK, BLOCK), :]
    wait(plane_in.at[0:15], recv_sem.at[0])
    total = plane_in[0]
    for n in range(1, 16):
        total = total + plane_in[n]
    plane_sum[...] = total

    for o in (2, 1, 3):
        send(plane_sum.at[rows(near_at(o) * PART, PART)], near_in.at[near], send_sem.at[1], recv_sem.at[1], near_device(o))
    near_in[near] = plane_sum[rows(near * PART, PART), :]
    wait(near_in.at[0:3], recv_sem.at[1])
    near_sum[...] = ((near_in[0] + near_in[1]) + near_in[2]) + near_in[3]

    far_in[far] = near_sum[...]
    for step in range(4):
        slot = (far - step) & 7
        src = near_sum if step == 0 else far_in.at[slot]
        send(src, far_in.at[slot], far_send.at[0, step], far_recv.at[0, step], up)
        if step < 3:
            slot = (far + step) & 7
            src = near_sum if step == 0 else far_in.at[slot]
            send(src, far_in.at[slot], far_send.at[1, step], far_recv.at[1, step], down)
        wait(near_sum, far_recv.at[0, step])
        if step < 3:
            wait(near_sum, far_recv.at[1, step])
    total = far_in[0]
    for n in range(1, 8):
        total = total + far_in[n]
    block = own + mine * BLOCK
    piece = full.at[rows(block + near * PART, PART)]
    piece[...] = total * (1.0 / replicas)

    for o in (2, 1, 3):
        send(piece, piece, send_sem.at[2], recv_sem.at[2], near_device(o))
    wait(full.at[0 : 3 * PART], recv_sem.at[2])
    piece = full.at[rows(block, BLOCK)]
    for i, j in offsets:
        send(piece, piece, send_sem.at[3], recv_sem.at[3], device(*plane(i, j), z, core))
    wait(full.at[0 : 15 * BLOCK], recv_sem.at[3])
    piece = full.at[rows(own, OWN)]
    send(piece, piece, core_send.at[4], core_recv.at[4], other)

    def gram_of(start):
        total = None
        for i in range(4):
            here = rows(start + i * CHUNK, CHUNK)
            value = jnp.concatenate(split(full[here, :]), axis=1)
            pieces[here, :] = value
            term = lax.dot_general(value, value, (((0,), (0,)), ((), ())), preferred_element_type=F32)
            total = term if total is None else total + term
        return total

    grams[core] = gram_of(own)
    wait(piece, core_recv.at[4])
    grams[1 - core] = gram_of(theirs)
    gram = grams[0] + grams[1]
    gram = (gram[0:128, 0:128] + gram[128:256, 128:256]) + (gram[0:128, 128:256] + gram[128:256, 0:128])
    gram = gram[0:RANK, :] + pltpu.roll(gram[RANK:128, :], RANK, 1)
    factor = inverse_factor(jnp.where(lanes < RANK, gram, jnp.where(lanes == at + RANK, 1.0, 0.0)))
    inverse = jnp.where(lanes < RANK, 0.0, factor)
    inverse = jnp.concatenate([pltpu.roll(inverse, RANK, 1), inverse], axis=0)
    high, low = split(inverse)
    weights = jnp.concatenate([jnp.concatenate([high, high], axis=1), jnp.concatenate([low, low], axis=1)], axis=0)

    right_sum = jnp.zeros((128, 2 * COLS), F32)
    for i in range(HALF // CHUNK):
        here = pl.ds(i * CHUNK, CHUNK)
        value = lax.dot_general(pieces[here, :], weights, (((1,), (1,)), ((), ())), preferred_element_type=F32)
        value = (value[:, 0:128] + value[:, 128:256]).astype(BF16)
        q[here, :] = value
        right_sum += lax.dot_general(value, comb[here, :], (((0,), (0,)), ((), ())), preferred_element_type=F32)
    right[...] = right_sum[0:RANK, 0:COLS] + right_sum[RANK:128, COLS : 2 * COLS]

    send(right.at[rows((1 - core) * 32, 32)], right_core, core_send.at[5], core_recv.at[5], other)
    q_copy = pltpu.make_async_copy(q, q_out, local_sem.at[3])
    q_copy.start()
    wait(right_core, core_recv.at[5])
    base = core * 32
    here = rows(base, 32)
    right[here, :] = right[here, :] + right_core[...]
    for i in (2, 1, 3):
        py = (y + i) & 3
        send(right.at[rows(base + py * 8, 8)], right_y.at[y], send_sem.at[4], recv_sem.at[4], device(x, py, z, core))
    right_y[y] = right[rows(base + y * 8, 8), :]
    wait(right_y.at[0:3], recv_sem.at[4])
    right_near_sum[0] = ((right_y[0] + right_y[1]) + right_y[2]) + right_y[3]
    right_near[near] = right_near_sum[0]
    for o in (2, 1, 3):
        send(right_near_sum.at[0], right_near.at[near], send_sem.at[5], recv_sem.at[5], near_device(o))
    wait(right_near.at[0:3], recv_sem.at[5])
    right_near_sum[1] = ((right_near[0] + right_near[1]) + right_near[2]) + right_near[3]
    line = far & 3
    right_far[line] = right_near_sum[1]
    for o in (2, 1, 3):
        send(right_near_sum.at[1], right_far.at[line], send_sem.at[6], recv_sem.at[6], in_line(o))
    wait(right_far.at[0:3], recv_sem.at[6])
    total = ((right_far[0] + right_far[1]) + right_far[2]) + right_far[3]
    piece = right_full.at[rows(base + y * 8, 8)]
    piece[...] = total * (1.0 / replicas)
    for i in (2, 1, 3):
        send(piece, piece, send_sem.at[7], recv_sem.at[7], device(x, (y + i) & 3, z, core))
    wait(right_full.at[0:24], recv_sem.at[7])
    piece = right_full.at[rows(base, 32)]
    send(piece, piece, core_send.at[6], core_recv.at[6], other)
    wait(piece, core_recv.at[6])
    right_out[...] = right_full[...]

    for i in range(4):
        wait(from_core.at[i], core_send.at[i])
    wait(full.at[0:OWN], core_send.at[4])
    wait(right_core, core_send.at[5])
    wait(right_core, core_send.at[6])
    wait(plane_in.at[0:15], send_sem.at[0])
    wait(near_in.at[0:3], send_sem.at[1])
    wait(near_in.at[0:3], send_sem.at[2])
    wait(full.at[0 : 15 * BLOCK], send_sem.at[3])
    for n in (4, 5, 6):
        wait(right_y.at[0:3], send_sem.at[n])
    wait(right_full.at[0:24], send_sem.at[7])
    for step in range(4):
        wait(near_sum, far_send.at[0, step])
        if step < 3:
            wait(near_sum, far_send.at[1, step])
    comb_copy.wait()
    q_copy.wait()


def finish_kernel(q, comb, right, approx, new_errors):
    full = jnp.dot(q[...], twice(right[...].astype(BF16)), preferred_element_type=F32)
    error = (comb[...].astype(F32) - full).astype(BF16)
    full = full.astype(BF16)
    for n in range(2):
        approx[n] = full[:, COLS * n : COLS * (n + 1)]
        new_errors[n] = error[:, COLS * n : COLS * (n + 1)]


def local(replicas, grads, errors, basis):
    vmem, dma = pltpu.VMEM, pltpu.SemaphoreType.DMA
    q, comb, right = pl.pallas_call(
        functools.partial(exchange_kernel, replicas),
        name="exchange",
        out_shape=(
            jax.ShapeDtypeStruct((HALF, 128), BF16),
            jax.ShapeDtypeStruct((HALF, 2 * COLS), BF16),
            jax.ShapeDtypeStruct((RANK, COLS), F32),
        ),
        in_specs=[pl.BlockSpec(memory_space=pl.ANY)] * 2 + [pl.BlockSpec(memory_space=vmem)],
        out_specs=(pl.BlockSpec(memory_space=pl.ANY),) * 2 + (pl.BlockSpec(memory_space=vmem),),
        scratch_shapes=[
            vmem((2 * HALF, COLS), BF16), vmem((2 * HALF, COLS), BF16), vmem((HALF, 2 * COLS), BF16),
            vmem((128, 2 * COLS), BF16), vmem((HALF, 128), F32), vmem((4, CHUNK, 128), F32),
            vmem((16, BLOCK, 128), F32), vmem((BLOCK, 128), F32), vmem((4, PART, 128), F32), vmem((PART, 128), F32),
            vmem((8, PART, 128), F32), vmem((HALF, 128), F32), vmem((HALF, 256), BF16), vmem((2, 256, 256), F32),
            vmem((HALF, 128), BF16),
            vmem((RANK, COLS), F32), vmem((32, COLS), F32), vmem((4, 8, COLS), F32), vmem((4, 8, COLS), F32),
            vmem((2, 8, COLS), F32), vmem((4, 8, COLS), F32), vmem((RANK, COLS), F32),
            dma((4,)), dma((7,)), dma((7,)), dma((8,)), dma((8,)), dma((2, 4)), dma((2, 4)),
        ],
        compiler_params=pltpu.CompilerParams(collective_id=0, has_side_effects=True, vmem_limit_bytes=56 << 20),
    )(grads, errors, basis.T)
    whole = pl.BlockSpec((RANK, COLS), lambda i: (0, 0))
    pair = pl.BlockSpec((2, 512, COLS), lambda i: (0, i, 0))
    approx, new_errors = pl.pallas_call(
        finish_kernel,
        name="finish",
        grid=(HALF // 512,),
        out_shape=(
            jax.ShapeDtypeStruct((2, HALF, COLS), BF16),
            jax.ShapeDtypeStruct((2, HALF, COLS), BF16),
        ),
        in_specs=[pl.BlockSpec((512, 128), lambda i: (i, 0)), pl.BlockSpec((512, 2 * COLS), lambda i: (i, 0)), whole],
        out_specs=(pair, pair),
    )(q, comb, right)
    return approx.reshape(2 * HALF, COLS), new_errors.reshape(1, 2 * HALF, COLS), right.T


def solution(mesh):
    placed = (P("dp", None, "tensor"), P("dp", None, "tensor"), P("tensor", None))
    return jax.shard_map(
        functools.partial(local, mesh.shape["dp"]),
        mesh=mesh,
        in_specs=placed,
        out_specs=(P(None, "tensor"), P("dp", None, "tensor"), P("tensor", None)),
        check_vma=False,
    )
```

time: 2410 us -> 105 us (0.04)
  blocking collectives: 1450 us -> 0 us
  waiting for transfers between devices: 904 us -> 0 us
  Pallas kernels: 0 us -> 103 us
    psum x1 -> x0, blocking collectives: 1450 us -> none  [local(): new_basis = lax.psum(right_part, 'dp') / replicas]
    psum x1 -> x0, waiting for transfers between devices: 904 us -> none  [local(): left_factor = lax.psum(left_part, ('dp', 'tensor')) / replicas]
    pallas_call x0 -> x2, Pallas kernels: none -> 103 us  [the longest x1 99.4 us: local(): pl.pallas_call(functools.partial(exchange_kernel, replicas), name='exchan...]
  transfers between devices with their start and end apart: 1 -> 0, of which waited for: 1 -> 0; matrix products, arithmetic and copies ran while one was open for 0% -> 0% of each run, Pallas kernels for 0% -> 0%
where the time goes in v1:
time: 105 us
  Pallas kernels  103 us (98%)
    pallas_call x1, Pallas kernels, local(): pl.pallas_call(functools.partial(exchange_kernel, replicas), name='exchan...  99.4 us
    pallas_call x1, Pallas kernels, local(): pl.pallas_call(finish_kernel, name='finish', grid=(HALF // 512,), out_sha...  4.09 us

profile of v1, /device:TPU:1, one launch (start us, length us, event | category | flops | bytes accessed | tf_op | source)
XLA Modules:
  0.0 104.8 jit_solution(11342234365068468725)
XLA Ops:
  0.6 99.4 %exchange.1 = (bf16[2048,128]{1,0:T(8,128)(2,1)}, bf16[2048,256]{1,0:T(8,128)(2,1)}, f32[64,128]{1,0:T(8,128)}) custom-call(bf16[1,4096,128]{2,1,0:T(8,128)(2,1)} %grads.1, bf16[1,4096,128]{2,1,0:T(8,128)(2,1)} %errors.1, f32[64,128]{1,0:T(8,128)} %bitcast.5), custom_call_target="tpu_custom_call" | custom-call | tf_op jit(solution)/shard_map/exchange/pallas_call | solution.py:288
  100.0 0.0 copy-start
  100.0 4.1 %finish.1 = (bf16[2,2048,128]{2,1,0:T(8,128)(2,1)}, bf16[2,2048,128]{2,1,0:T(8,128)(2,1)}) custom-call(bf16[2048,128]{1,0:T(8,128)(2,1)} %get-tuple-element.8.q, bf16[2048,256]{1,0:T(8,128)(2,1)} %get-tuple-element.9.comb, f32[64,128]{1,0:T(8,128)} %get-tuple-element.10.right), custom_call_target="tpu_custom_call" | custom-call | tf_op jit(solution)/shard_map/finish/pallas_call | solution.py:312
  104.1 0.0 copy-done
  104.1 0.6 copy.7
Async XLA Ops:
  100.0 4.1 %copy-start = (f32[64,128]{1,0:T(8,128)S(1)}, f32[64,128]{1,0:T(8,128)}, u32[]{:S(2)}) copy-start(f32[64,128]{1,0:T(8,128)} %get-tuple-element.10.right) | copy-start | bytes 98308

commit v2 on v1

v2 whole, which is shorter than its diff:
```python
import functools

import jax
import jax.numpy as jnp
from jax import lax
from jax.experimental import pallas as pl
from jax.experimental.pallas import tpu as pltpu
from jax.sharding import PartitionSpec as P

MESH = pl.DeviceIdType.MESH
F32, BF16 = jnp.float32, jnp.bfloat16
COLS, RANK = 128, 64
HALF = 2048
OWN = 1024
BLOCK = 64
PART = 16
CHUNK = 256


def device(x, y, z, core):
    return ((z & 15) * 8 + y * 2 + core, (z >> 4) * 4 + x)


def rows(start, size):
    return pl.ds(pl.multiple_of(start, size), size)


def send(src, dst, send_sem, recv_sem, to):
    copy = pltpu.make_async_remote_copy(
        src_ref=src, dst_ref=dst, send_sem=send_sem, recv_sem=recv_sem, device_id=to, device_id_type=MESH
    )
    copy.start()


def wait(ref, sem):
    pltpu.make_async_copy(ref, ref, sem).wait()


def split(value):
    high = value.astype(BF16)
    low = (value - high.astype(F32)).astype(BF16)
    return high, low


def twice(value):
    zeros = jnp.zeros_like(value)
    return jnp.concatenate(
        [jnp.concatenate([value, zeros], axis=1), jnp.concatenate([zeros, value], axis=1)], axis=0
    )


def inverse_factor(gram):
    tiles = RANK // 8
    rows_at = lax.broadcasted_iota(jnp.int32, (8, 128), 0)
    m = [gram[8 * b : 8 * b + 8, :] for b in range(tiles)]
    pivots = []
    for k in range(RANK):
        at, sub = divmod(k, 8)
        pivot_row = m[at][sub : sub + 1, :]
        pivot = pivot_row[:, k : k + 1]
        pivots.append(pivot)
        scaled = pivot_row * (1.0 / pivot)
        for b in range(at, tiles):
            update = m[b][:, k : k + 1] * scaled
            if b == at:
                update = jnp.where(rows_at > sub, update, 0.0)
            m[b] = m[b] - update
    out = []
    for b in range(tiles):
        scale = jnp.concatenate(pivots[8 * b : 8 * b + 8], axis=0)
        out.append(m[b] * lax.rsqrt(scale))
    return jnp.concatenate(out, axis=0)


def exchange_kernel(
    replicas, grads, errors, basis, q_out, comb_out, right_out,
    g_in, e_in, comb, blocks, part, from_core, plane_in, plane_sum, near_in, near_sum, far_in, full, mates, pieces, grams,
    q, right, right_in, right_near, right_near_sum, right_far, right_full,
    local_sem, core_send, core_recv, send_sem, recv_sem, far_send, far_recv,
):
    d, t = lax.axis_index("dp"), lax.axis_index("tensor")
    core, y, z, x = d & 1, (d >> 1) & 3, (t >> 2) * 16 + (d >> 3), t & 3
    near, far, mine = z & 3, z >> 2, y * 4 + x
    other = device(x, y, z, 1 - core)
    own, theirs = core * OWN, (1 - core) * OWN

    def plane(i, j):
        return (x + j) & 3, (y + i) & 3

    def near_at(o):
        return (near + o) & 3

    def near_device(o, j=0):
        return device((x + j) & 3, y, (z & 28) | near_at(o), core)

    def in_line(o):
        return device(x, y, (z & 19) | (((far + o) & 3) << 2), core)

    def in_ring(o):
        return device(x, y, (z + 4 * o) & 31, core)

    def mate(c, i):
        to_core, to_y = core ^ c, (y + i) & 3
        return to_core * 4 + to_y, device(x, to_y, z, to_core)

    offsets = [(i, j) for i in range(4) for j in range(4) if (i, j) != (0, 0)]
    mate_offsets = [(0, 2), (1, 2), (0, 1), (0, 3), (1, 1), (1, 3), (1, 0)]
    ring_offsets = [2, -2, 1, -1]

    for n, start in enumerate((theirs, own)):
        for base in (0, HALF):
            here = rows(base + start, OWN)
            pltpu.make_async_copy(grads.at[0, here], g_in.at[here], local_sem.at[n]).start()
            pltpu.make_async_copy(errors.at[0, here], e_in.at[here], local_sem.at[n]).start()

    barrier = pltpu.get_barrier_semaphore()
    partners = [in_ring(o) for o in ring_offsets] + [near_device(o) for o in (1, 2, 3)]
    partners += [device(*plane(i, j), z, core) for i, j in offsets] + [other]
    for to in partners:
        pl.semaphore_signal(barrier, inc=1, device_id=to, device_id_type=MESH)

    blocks[...] = twice(basis[...].astype(BF16))
    lanes = lax.broadcasted_iota(jnp.int32, (RANK, 128), 1)
    at = lax.broadcasted_iota(jnp.int32, (RANK, 128), 0)

    def product(start):
        both = []
        for base in (0, HALF):
            here = rows(base + start, CHUNK)
            both.append((g_in[here, :].astype(F32) + e_in[here, :].astype(F32)).astype(BF16))
        value = jnp.concatenate(both, axis=1)
        comb[rows(start, CHUNK), :] = value
        part[rows(start, CHUNK), :] = lax.dot_general(
            value, blocks[...], (((1,), (1,)), ((), ())), preferred_element_type=F32
        )

    order = [((y + i) & 3) * CHUNK for i in range(4)]
    wait(g_in, local_sem.at[0])
    for i in range(4):
        product(theirs + order[i])
    pl.semaphore_wait(barrier, len(partners))
    for i in range(4):
        send(part.at[rows(theirs + order[i], CHUNK)], from_core.at[i], core_send.at[i], core_recv.at[i], other)
    wait(g_in, local_sem.at[1])
    for i in range(4):
        product(own + order[i])
    for i in range(4):
        wait(from_core.at[i], core_recv.at[i])
        here = rows(own + order[i], CHUNK)
        part[here, :] = part[here, :] + from_core[i]
        for j in range(4):
            if (i, j) != (0, 0):
                px, py = plane(i, j)
                src = part.at[rows(own + (py * 4 + px) * BLOCK, BLOCK)]
                send(src, plane_in.at[mine], send_sem.at[0], recv_sem.at[0], device(px, py, z, core))
    comb_copy = pltpu.make_async_copy(comb, comb_out, local_sem.at[2])
    comb_copy.start()
    plane_in[mine] = part[rows(own + mine * BLOCK, BLOCK), :]
    wait(plane_in.at[0:15], recv_sem.at[0])
    total = plane_in[0]
    for n in range(1, 16):
        total = total + plane_in[n]
    plane_sum[...] = total

    for o in (2, 1, 3):
        send(plane_sum.at[rows(near_at(o) * PART, PART)], near_in.at[near], send_sem.at[1], recv_sem.at[1], near_device(o))
    for n, (c, i) in enumerate(mate_offsets):
        index, to = mate(c, i)
        send(comb.at[rows(index * CHUNK, CHUNK)], mates.at[n], send_sem.at[2], recv_sem.at[2], to)
    near_in[near] = plane_sum[rows(near * PART, PART), :]
    wait(near_in.at[0:3], recv_sem.at[1])
    near_sum[...] = ((near_in[0] + near_in[1]) + near_in[2]) + near_in[3]

    for n, o in enumerate(ring_offsets):
        send(near_sum, far_in.at[far], far_send.at[n], far_recv.at[n], in_ring(o))
    far_in[far] = near_sum[...]
    above, below = far_in.at[(far + 2) & 7], far_in.at[(far - 2) & 7]
    wait(near_sum, far_recv.at[1])
    send(above, above, far_send.at[4], far_recv.at[4], in_ring(-2))
    send(above, above, far_send.at[5], far_recv.at[5], in_ring(-1))
    wait(near_sum, far_recv.at[0])
    send(below, below, far_send.at[6], far_recv.at[6], in_ring(1))
    for n in (2, 3, 5, 6, 4):
        wait(near_sum, far_recv.at[n])
    total = far_in[0]
    for n in range(1, 8):
        total = total + far_in[n]
    slab = own + y * CHUNK
    piece = full.at[rows(slab + x * BLOCK + near * PART, PART)]
    piece[...] = total * (1.0 / replicas)
    for o in (2, 1, 3, 0):
        for j in (2, 1, 3, 0):
            if (o, j) != (0, 0):
                send(piece, piece, send_sem.at[3], recv_sem.at[3], near_device(o, j))
    wait(mates.at[0:7], recv_sem.at[2])
    wait(full.at[0 : 15 * PART], recv_sem.at[3])

    value = jnp.concatenate(split(full[rows(slab, CHUNK), :]), axis=1)
    total = lax.dot_general(value, comb[rows(slab, CHUNK), :], (((0,), (0,)), ((), ())), preferred_element_type=F32)
    for n in range(7):
        total = total + lax.dot_general(value, mates[n], (((0,), (0,)), ((), ())), preferred_element_type=F32)
    right[...] = (total[0:64, 0:COLS] + total[128:192, 0:COLS]) + (total[64:128, COLS:] + total[192:256, COLS:])
    for n, (c, i) in enumerate(mate_offsets):
        index, to = mate(c, i)
        send(right.at[rows(index * 8, 8)], right_in.at[n], send_sem.at[4], recv_sem.at[4], to)
    piece = full.at[rows(slab, CHUNK)]
    for i in (2, 1, 3):
        send(piece, piece, send_sem.at[5], recv_sem.at[5], device(x, (y + i) & 3, z, core))
    lot = rows((core * 4 + y) * 8, 8)
    wait(right_in, recv_sem.at[4])
    total = right[lot, :]
    for n in range(7):
        total = total + right_in[n]
    right_near_sum[0] = total
    for o in (2, 1, 3):
        send(right_near_sum.at[0], right_near.at[near], send_sem.at[6], recv_sem.at[6], near_device(o))
    right_near[near] = right_near_sum[0]
    wait(full.at[0 : 3 * CHUNK], recv_sem.at[5])
    half = full.at[rows(own, OWN)]
    send(half, half, core_send.at[4], core_recv.at[4], other)

    def gram_of(start):
        total = None
        for i in range(4):
            here = rows(start + i * CHUNK, CHUNK)
            value = jnp.concatenate(split(full[here, :]), axis=1)
            pieces[here, :] = value
            term = lax.dot_general(value, value, (((0,), (0,)), ((), ())), preferred_element_type=F32)
            total = term if total is None else total + term
        return total

    wait(right_near.at[0:3], recv_sem.at[6])
    right_near_sum[1] = ((right_near[0] + right_near[1]) + right_near[2]) + right_near[3]
    line = far & 3
    for o in (2, 1, 3):
        send(right_near_sum.at[1], right_far.at[line], send_sem.at[7], recv_sem.at[7], in_line(o))
    right_far[line] = right_near_sum[1]
    grams[core] = gram_of(own)
    wait(half, core_recv.at[4])
    grams[1 - core] = gram_of(theirs)
    gram = grams[0] + grams[1]
    gram = (gram[0:128, 0:128] + gram[128:256, 128:256]) + (gram[0:128, 128:256] + gram[128:256, 0:128])
    gram = gram[0:RANK, :] + pltpu.roll(gram[RANK:128, :], RANK, 1)
    factor = inverse_factor(jnp.where(lanes < RANK, gram, jnp.where(lanes == at + RANK, 1.0, 0.0)))
    inverse = jnp.where(lanes < RANK, 0.0, factor)
    left_inverse = pltpu.roll(inverse, RANK, 1)

    wait(right_far.at[0:3], recv_sem.at[7])
    total = ((right_far[0] + right_far[1]) + right_far[2]) + right_far[3]
    piece = right_full.at[lot]
    piece[...] = total * (1.0 / replicas)
    for c, i in mate_offsets:
        send(piece, piece, send_sem.at[8], recv_sem.at[8], mate(c, i)[1])

    high, low = split(jnp.concatenate([left_inverse, inverse], axis=0))
    weights = jnp.concatenate([jnp.concatenate([high, high], axis=1), jnp.concatenate([low, low], axis=1)], axis=0)
    for i in range(HALF // CHUNK):
        here = pl.ds(i * CHUNK, CHUNK)
        value = lax.dot_general(pieces[here, :], weights, (((1,), (1,)), ((), ())), preferred_element_type=F32)
        q[here, :] = (value[:, 0:128] + value[:, 128:256]).astype(BF16)
    q_copy = pltpu.make_async_copy(q, q_out, local_sem.at[3])
    q_copy.start()
    wait(right_full.at[0:56], recv_sem.at[8])
    right_out[...] = jnp.dot(
        left_inverse[:, 0:RANK], right_full[...], precision=lax.Precision.HIGHEST, preferred_element_type=F32
    )

    for i in range(4):
        wait(from_core.at[i], core_send.at[i])
    wait(half, core_send.at[4])
    wait(plane_in.at[0:15], send_sem.at[0])
    wait(near_in.at[0:3], send_sem.at[1])
    wait(mates.at[0:7], send_sem.at[2])
    wait(full.at[0 : 15 * PART], send_sem.at[3])
    wait(right_in, send_sem.at[4])
    wait(full.at[0 : 3 * CHUNK], send_sem.at[5])
    wait(right_near.at[0:3], send_sem.at[6])
    wait(right_near.at[0:3], send_sem.at[7])
    wait(right_in, send_sem.at[8])
    for n in range(7):
        wait(near_sum, far_send.at[n])
    comb_copy.wait()
    q_copy.wait()


def finish_kernel(q, comb, right, approx, new_errors, approx_out, errors_out, sem):
    weights = twice(right[...].astype(BF16))
    copies = []
    for i in range(HALF // 512):
        here = pl.ds(i * 512, 512)
        full = jnp.dot(q[here, :], weights, preferred_element_type=F32)
        error = (comb[here, :].astype(F32) - full).astype(BF16)
        full = full.astype(BF16)
        for n in range(2):
            approx_out[n, here, :] = full[:, COLS * n : COLS * (n + 1)]
            errors_out[n, here, :] = error[:, COLS * n : COLS * (n + 1)]
        for n, (src, dst) in enumerate(((approx_out, approx), (errors_out, new_errors))):
            copies.append(pltpu.make_async_copy(src.at[:, here], dst.at[:, here], sem.at[n, i]))
            copies[-1].start()
    for copy in copies:
        copy.wait()


def local(replicas, grads, errors, basis):
    vmem, dma = pltpu.VMEM, pltpu.SemaphoreType.DMA
    anywhere, inside = pl.BlockSpec(memory_space=pl.ANY), pl.BlockSpec(memory_space=vmem)
    q, comb, right = pl.pallas_call(
        functools.partial(exchange_kernel, replicas),
        name="exchange",
        out_shape=(
            jax.ShapeDtypeStruct((HALF, 128), BF16),
            jax.ShapeDtypeStruct((HALF, 2 * COLS), BF16),
            jax.ShapeDtypeStruct((RANK, COLS), F32),
        ),
        in_specs=[pl.BlockSpec(memory_space=pltpu.HBM)] * 2 + [inside],
        out_specs=(anywhere, anywhere, inside),
        scratch_shapes=[
            vmem((2 * HALF, COLS), BF16), vmem((2 * HALF, COLS), BF16), vmem((HALF, 2 * COLS), BF16),
            vmem((128, 2 * COLS), BF16), vmem((HALF, 128), F32), vmem((4, CHUNK, 128), F32),
            vmem((16, BLOCK, 128), F32), vmem((BLOCK, 128), F32), vmem((4, PART, 128), F32), vmem((PART, 128), F32),
            vmem((8, PART, 128), F32), vmem((HALF, 128), F32), vmem((7, CHUNK, 2 * COLS), BF16),
            vmem((HALF, 256), BF16), vmem((2, 256, 256), F32), vmem((HALF, 128), BF16),
            vmem((RANK, COLS), F32), vmem((7, 8, COLS), F32), vmem((4, 8, COLS), F32),
            vmem((2, 8, COLS), F32), vmem((4, 8, COLS), F32), vmem((RANK, COLS), F32),
            dma((4,)), dma((5,)), dma((5,)), dma((9,)), dma((9,)), dma((7,)), dma((7,)),
        ],
        compiler_params=pltpu.CompilerParams(collective_id=0, has_side_effects=True, vmem_limit_bytes=20 << 20),
    )(grads, errors, basis.T)
    approx, new_errors = pl.pallas_call(
        finish_kernel,
        name="finish",
        out_shape=(jax.ShapeDtypeStruct((2, HALF, COLS), BF16),) * 2,
        in_specs=[inside] * 3,
        out_specs=(anywhere,) * 2,
        scratch_shapes=[vmem((2, HALF, COLS), BF16), vmem((2, HALF, COLS), BF16), dma((2, 4))],
        compiler_params=pltpu.CompilerParams(vmem_limit_bytes=16 << 20),
    )(q, comb, right)
    return approx.reshape(2 * HALF, COLS), new_errors.reshape(1, 2 * HALF, COLS), right.T


def solution(mesh):
    placed = (P("dp", None, "tensor"), P("dp", None, "tensor"), P("tensor", None))
    return jax.shard_map(
        functools.partial(local, mesh.shape["dp"]),
        mesh=mesh,
        in_specs=placed,
        out_specs=(P(None, "tensor"), P("dp", None, "tensor"), P("tensor", None)),
        check_vma=False,
    )
```

time: 105 us -> 87.7 us (0.84)
  Pallas kernels: 103 us -> 82.9 us
  local copies, waits for them, and re-layouts: 0.62 us -> 3.82 us
    pallas_call x1, Pallas kernels: 99.4 us -> 81.2 us  [local(): pl.pallas_call(functools.partial(exchange_kernel, replicas), name='exchan...]
    unnamed x3 -> x7, local copies, waits for them, and re-layouts: 0.62 us -> 3.82 us
    pallas_call x1, Pallas kernels: 4.09 us -> 1.66 us  [local(): pl.pallas_call(finish_kernel, name='finish', out_shape=(jax.ShapeDtypeStr...]
where the time goes in v2:
time: 87.7 us; the launch traced here: 87.4 us
  Pallas kernels  82.9 us (95%)
  local copies, waits for them, and re-layouts  3.82 us (4%)
    pallas_call x1, Pallas kernels, local(): pl.pallas_call(functools.partial(exchange_kernel, replicas), name='exchan...  81.2 us
    unnamed x7, local copies, waits for them, and re-layouts  3.82 us

profile of v2, /device:TPU:1, one launch (start us, length us, event | category | flops | bytes accessed | tf_op | source)
XLA Modules:
  0.0 87.4 jit_solution(13369654337963625902)
XLA Ops:
  0.6 0.0 copy-start
  0.6 1.2 %copy-done = bf16[1,4096,128]{2,1,0:T(8,128)(2,1)S(1)} copy-done((bf16[1,4096,128]{2,1,0:T(8,128)(2,1)S(1)}, bf16[1,4096,128]{2,1,0:T(8,128)(2,1)}, u32[]{:S(2)}) %copy-start) | copy-done | bytes 1048600
  1.9 0.0 copy-start.1
  1.9 1.2 %copy-done.1 = bf16[1,4096,128]{2,1,0:T(8,128)(2,1)S(1)} copy-done((bf16[1,4096,128]{2,1,0:T(8,128)(2,1)S(1)}, bf16[1,4096,128]{2,1,0:T(8,128)(2,1)}, u32[]{:S(2)}) %copy-start.1) | copy-done | bytes 1048600
  3.1 0.0 copy-start.2
  3.1 0.8 copy-done.2
  3.8 81.2 %exchange.1 = (bf16[2048,128]{1,0:T(8,128)(2,1)S(1)}, bf16[2048,256]{1,0:T(8,128)(2,1)S(1)}, f32[64,128]{1,0:T(8,128)S(1)}) custom-call(bf16[1,4096,128]{2,1,0:T(8,128)(2,1)S(1)} %copy-done, bf16[1,4096,128]{2,1,0:T(8,128)(2,1)S(1)} %copy-done.1, f32[64,128]{1,0:T(8,128)S(1)} %bitcast.5), custom_call_target="tpu_custom_call" | custom-call | tf_op jit(solution)/shard_map/exchange/pallas_call | solution.py:307
  85.1 1.7 %finish.1 = (bf16[2,2048,128]{2,1,0:T(8,128)(2,1)}, bf16[2,2048,128]{2,1,0:T(8,128)(2,1)}) custom-call(bf16[2048,128]{1,0:T(8,128)(2,1)S(1)} %get-tuple-element.8.q, bf16[2048,256]{1,0:T(8,128)(2,1)S(1)} %get-tuple-element.9.comb, f32[64,128]{1,0:T(8,128)S(1)} %get-tuple-element.10.right), custom_call_target="tpu_custom_call" | custom-call | tf_op jit(solution)/shard_map/finish/pallas_call | solution.py:329
  86.8 0.6 copy.7
Async XLA Ops:
  0.6 1.2 %copy-start = (bf16[1,4096,128]{2,1,0:T(8,128)(2,1)S(1)}, bf16[1,4096,128]{2,1,0:T(8,128)(2,1)}, u32[]{:S(2)}) copy-start(bf16[1,4096,128]{2,1,0:T(8,128)(2,1)} %grads.1) | copy-start | bytes 3145732
  1.9 1.2 %copy-start.1 = (bf16[1,4096,128]{2,1,0:T(8,128)(2,1)S(1)}, bf16[1,4096,128]{2,1,0:T(8,128)(2,1)}, u32[]{:S(2)}) copy-start(bf16[1,4096,128]{2,1,0:T(8,128)(2,1)} %errors.1) | copy-start | bytes 3145732
  3.1 0.8 copy-start.2

commit v3 on v2

--- a/solution.py
+++ b/solution.py
@@ -76,7 +76,7 @@
     replicas, grads, errors, basis, q_out, comb_out, right_out,
     g_in, e_in, comb, blocks, part, from_core, plane_in, plane_sum, near_in, near_sum, far_in, full, mates, pieces, grams,
     q, right, right_in, right_near, right_near_sum, right_far, right_full,
-    local_sem, core_send, core_recv, send_sem, recv_sem, far_send, far_recv,
+    local_sem, core_send, core_recv, send_sem, recv_sem, far_send, far_recv, tokens,
 ):
     d, t = lax.axis_index("dp"), lax.axis_index("tensor")
     core, y, z, x = d & 1, (d >> 1) & 3, (t >> 2) * 16 + (d >> 3), t & 3
@@ -113,11 +113,17 @@
             pltpu.make_async_copy(grads.at[0, here], g_in.at[here], local_sem.at[n]).start()
             pltpu.make_async_copy(errors.at[0, here], e_in.at[here], local_sem.at[n]).start()
 
+    def along(o):
+        return device(x, y, (z + o) & 31, core)
+
+    def signal(sem, partners):
+        for to in partners:
+            pl.semaphore_signal(sem, inc=1, device_id=to, device_id_type=MESH)
+
     barrier = pltpu.get_barrier_semaphore()
-    partners = [in_ring(o) for o in ring_offsets] + [near_device(o) for o in (1, 2, 3)]
-    partners += [device(*plane(i, j), z, core) for i, j in offsets] + [other]
-    for to in partners:
-        pl.semaphore_signal(barrier, inc=1, device_id=to, device_id_type=MESH)
+    line_x = [device(*plane(0, j), z, core) for j in (2, 1, 3)]
+    line_y = [device(*plane(i, 0), z, core) for i in (2, 1, 3)]
+    signal(barrier, line_x + line_y + [along(1), along(31), other])
 
     blocks[...] = twice(basis[...].astype(BF16))
     lanes = lax.broadcasted_iota(jnp.int32, (RANK, 128), 1)
@@ -138,12 +144,17 @@
     wait(g_in, local_sem.at[0])
     for i in range(4):
         product(theirs + order[i])
-    pl.semaphore_wait(barrier, len(partners))
+    pl.semaphore_wait(barrier, 9)
+    signal(tokens.at[0], line_x)
+    signal(tokens.at[1], [along(1), along(31)])
     for i in range(4):
         send(part.at[rows(theirs + order[i], CHUNK)], from_core.at[i], core_send.at[i], core_recv.at[i], other)
     wait(g_in, local_sem.at[1])
     for i in range(4):
         product(own + order[i])
+    pl.semaphore_wait(tokens.at[0], 3)
+    pl.semaphore_wait(tokens.at[1], 2)
+    signal(tokens.at[2], [along(2), along(30)])
     for i in range(4):
         wait(from_core.at[i], core_recv.at[i])
         here = rows(own + order[i], CHUNK)
@@ -156,6 +167,8 @@
     comb_copy = pltpu.make_async_copy(comb, comb_out, local_sem.at[2])
     comb_copy.start()
     plane_in[mine] = part[rows(own + mine * BLOCK, BLOCK), :]
+    pl.semaphore_wait(tokens.at[2], 2)
+    signal(tokens.at[3], [along(4), along(28)])
     wait(plane_in.at[0:15], recv_sem.at[0])
     total = plane_in[0]
     for n in range(1, 16):
@@ -171,6 +184,7 @@
     wait(near_in.at[0:3], recv_sem.at[1])
     near_sum[...] = ((near_in[0] + near_in[1]) + near_in[2]) + near_in[3]
 
+    pl.semaphore_wait(tokens.at[3], 2)
     for n, o in enumerate(ring_offsets):
         send(near_sum, far_in.at[far], far_send.at[n], far_recv.at[n], in_ring(o))
     far_in[far] = near_sum[...]
@@ -283,9 +297,10 @@
     q_copy.wait()
 
 
-def finish_kernel(q, comb, right, approx, new_errors, approx_out, errors_out, sem):
+def finish_kernel(q, comb, right, approx, new_errors, new_basis, approx_out, errors_out, sem, basis_sem):
     weights = twice(right[...].astype(BF16))
-    copies = []
+    copies = [pltpu.make_async_copy(right, new_basis, basis_sem)]
+    copies[0].start()
     for i in range(HALF // 512):
         here = pl.ds(i * 512, 512)
         full = jnp.dot(q[here, :], weights, preferred_element_type=F32)
@@ -312,7 +327,7 @@
             jax.ShapeDtypeStruct((HALF, 2 * COLS), BF16),
             jax.ShapeDtypeStruct((RANK, COLS), F32),
         ),
-        in_specs=[pl.BlockSpec(memory_space=pltpu.HBM)] * 2 + [inside],
+        in_specs=[anywhere] * 2 + [inside],
         out_specs=(anywhere, anywhere, inside),
         scratch_shapes=[
             vmem((2 * HALF, COLS), BF16), vmem((2 * HALF, COLS), BF16), vmem((HALF, 2 * COLS), BF16),
@@ -323,19 +338,20 @@
             vmem((RANK, COLS), F32), vmem((7, 8, COLS), F32), vmem((4, 8, COLS), F32),
             vmem((2, 8, COLS), F32), vmem((4, 8, COLS), F32), vmem((RANK, COLS), F32),
             dma((4,)), dma((5,)), dma((5,)), dma((9,)), dma((9,)), dma((7,)), dma((7,)),
+            pltpu.SemaphoreType.REGULAR((4,)),
         ],
-        compiler_params=pltpu.CompilerParams(collective_id=0, has_side_effects=True, vmem_limit_bytes=20 << 20),
+        compiler_params=pltpu.CompilerParams(collective_id=0, has_side_effects=True, vmem_limit_bytes=52 << 20),
     )(grads, errors, basis.T)
-    approx, new_errors = pl.pallas_call(
+    approx, new_errors, new_basis = pl.pallas_call(
         finish_kernel,
         name="finish",
-        out_shape=(jax.ShapeDtypeStruct((2, HALF, COLS), BF16),) * 2,
+        out_shape=(jax.ShapeDtypeStruct((2, HALF, COLS), BF16),) * 2 + (jax.ShapeDtypeStruct((RANK, COLS), F32),),
         in_specs=[inside] * 3,
-        out_specs=(anywhere,) * 2,
-        scratch_shapes=[vmem((2, HALF, COLS), BF16), vmem((2, HALF, COLS), BF16), dma((2, 4))],
+        out_specs=(anywhere,) * 3,
+        scratch_shapes=[vmem((2, HALF, COLS), BF16), vmem((2, HALF, COLS), BF16), dma((2, 4)), dma],
         compiler_params=pltpu.CompilerParams(vmem_limit_bytes=16 << 20),
     )(q, comb, right)
-    return approx.reshape(2 * HALF, COLS), new_errors.reshape(1, 2 * HALF, COLS), right.T
+    return approx.reshape(2 * HALF, COLS), new_errors.reshape(1, 2 * HALF, COLS), new_basis.T
 
 
 def solution(mesh):

time: 87.7 us -> 80.7 us (0.920)
  Pallas kernels: 82.9 us -> 79.1 us
  local copies, waits for them, and re-layouts: 3.82 us -> 0.75 us
    pallas_call x1, Pallas kernels: 81.2 us -> 77.4 us  [local(): pl.pallas_call(functools.partial(exchange_kernel, replicas), name='exchan...]
    unnamed x7 -> x2, local copies, waits for them, and re-layouts: 3.82 us -> 0.75 us
where the time goes in v3:
time: 80.7 us; the launch traced here: 80.4 us
  Pallas kernels  79.1 us (98%)
    pallas_call x1, Pallas kernels, local(): pl.pallas_call(functools.partial(exchange_kernel, replicas), name='exchan...  77.4 us
    pallas_call x1, Pallas kernels, local(): pl.pallas_call(finish_kernel, name='finish', out_shape=(jax.ShapeDtypeStr...  1.67 us

profile of v3, /device:TPU:1, one launch (start us, length us, event | category | flops | bytes accessed | tf_op | source)
XLA Modules:
  0.0 80.4 jit_solution(11129310410952278625)
XLA Ops:
  0.6 0.0 copy-start
  0.6 0.7 copy-done
  1.4 77.4 %exchange.1 = (bf16[2048,128]{1,0:T(8,128)(2,1)S(1)}, bf16[2048,256]{1,0:T(8,128)(2,1)S(1)}, f32[64,128]{1,0:T(8,128)S(1)}) custom-call(bf16[1,4096,128]{2,1,0:T(8,128)(2,1)} %grads.1, bf16[1,4096,128]{2,1,0:T(8,128)(2,1)} %errors.1, f32[64,128]{1,0:T(8,128)S(1)} %bitcast.4), custom_call_target="tpu_custom_call" | custom-call | tf_op jit(solution)/shard_map/exchange/pallas_call | solution.py:322
  78.8 1.7 %finish.1 = (bf16[2,2048,128]{2,1,0:T(8,128)(2,1)}, bf16[2,2048,128]{2,1,0:T(8,128)(2,1)}, f32[64,128]{1,0:T(8,128)}) custom-call(bf16[2048,128]{1,0:T(8,128)(2,1)S(1)} %get-tuple-element.9.q, bf16[2048,256]{1,0:T(8,128)(2,1)S(1)} %get-tuple-element.10.comb, f32[64,128]{1,0:T(8,128)S(1)} %get-tuple-element.11.right), custom_call_target="tpu_custom_call" | custom-call | tf_op jit(solution)/shard_map/finish/pallas_call | solution.py:345
Async XLA Ops:
  0.6 0.8 copy-start

commit v4 on v3

--- a/solution.py
+++ b/solution.py
@@ -74,8 +74,8 @@
 
 def exchange_kernel(
     replicas, grads, errors, basis, q_out, comb_out, right_out,
-    g_in, e_in, comb, blocks, part, from_core, plane_in, plane_sum, near_in, near_sum, far_in, full, mates, pieces, grams,
-    q, right, right_in, right_near, right_near_sum, right_far, right_full,
+    g_in, e_in, comb, blocks, part, from_core, plane_in, plane_sum, near_in, near_sum, far_in, full, mates, mate_sum, pieces, grams,
+    q, right, right_in, right_sum, right_far, right_full,
     local_sem, core_send, core_recv, send_sem, recv_sem, far_send, far_recv, tokens,
 ):
     d, t = lax.axis_index("dp"), lax.axis_index("tensor")
@@ -107,23 +107,22 @@
     mate_offsets = [(0, 2), (1, 2), (0, 1), (0, 3), (1, 1), (1, 3), (1, 0)]
     ring_offsets = [2, -2, 1, -1]
 
+    def along(o):
+        return device(x, y, (z + o) & 31, core)
+
+    def signal(sem, partners):
+        for to in partners:
+            pl.semaphore_signal(sem, inc=1, device_id=to, device_id_type=MESH)
+
+    barrier = pltpu.get_barrier_semaphore()
+    line_x = [device(*plane(0, j), z, core) for j in (2, 1, 3)]
+    line_y = [device(*plane(i, 0), z, core) for i in (2, 1, 3)]
+    signal(barrier, line_x + line_y + [along(1), along(31), other])
     for n, start in enumerate((theirs, own)):
         for base in (0, HALF):
             here = rows(base + start, OWN)
             pltpu.make_async_copy(grads.at[0, here], g_in.at[here], local_sem.at[n]).start()
             pltpu.make_async_copy(errors.at[0, here], e_in.at[here], local_sem.at[n]).start()
-
-    def along(o):
-        return device(x, y, (z + o) & 31, core)
-
-    def signal(sem, partners):
-        for to in partners:
-            pl.semaphore_signal(sem, inc=1, device_id=to, device_id_type=MESH)
-
-    barrier = pltpu.get_barrier_semaphore()
-    line_x = [device(*plane(0, j), z, core) for j in (2, 1, 3)]
-    line_y = [device(*plane(i, 0), z, core) for i in (2, 1, 3)]
-    signal(barrier, line_x + line_y + [along(1), along(31), other])
 
     blocks[...] = twice(basis[...].astype(BF16))
     lanes = lax.broadcasted_iota(jnp.int32, (RANK, 128), 1)
@@ -152,9 +151,6 @@
     wait(g_in, local_sem.at[1])
     for i in range(4):
         product(own + order[i])
-    pl.semaphore_wait(tokens.at[0], 3)
-    pl.semaphore_wait(tokens.at[1], 2)
-    signal(tokens.at[2], [along(2), along(30)])
     for i in range(4):
         wait(from_core.at[i], core_recv.at[i])
         here = rows(own + order[i], CHUNK)
@@ -164,6 +160,10 @@
                 px, py = plane(i, j)
                 src = part.at[rows(own + (py * 4 + px) * BLOCK, BLOCK)]
                 send(src, plane_in.at[mine], send_sem.at[0], recv_sem.at[0], device(px, py, z, core))
+        if i == 0:
+            pl.semaphore_wait(tokens.at[0], 3)
+            pl.semaphore_wait(tokens.at[1], 2)
+            signal(tokens.at[2], [along(2), along(30)])
     comb_copy = pltpu.make_async_copy(comb, comb_out, local_sem.at[2])
     comb_copy.start()
     plane_in[mine] = part[rows(own + mine * BLOCK, BLOCK), :]
@@ -194,44 +194,43 @@
     send(above, above, far_send.at[5], far_recv.at[5], in_ring(-1))
     wait(near_sum, far_recv.at[0])
     send(below, below, far_send.at[6], far_recv.at[6], in_ring(1))
+    slab = own + y * CHUNK
+    wait(mates.at[0:7], recv_sem.at[2])
+    for i in range(4):
+        here = pl.ds(i * 64, 64)
+        total = comb[rows(slab + i * 64, 64), :].astype(F32)
+        for n in range(7):
+            total = total + mates[n, here, :].astype(F32)
+        mate_sum[here, 0 : 2 * COLS], mate_sum[here, 2 * COLS :] = split(total)
     for n in (2, 3, 5, 6, 4):
         wait(near_sum, far_recv.at[n])
     total = far_in[0]
     for n in range(1, 8):
         total = total + far_in[n]
-    slab = own + y * CHUNK
     piece = full.at[rows(slab + x * BLOCK + near * PART, PART)]
     piece[...] = total * (1.0 / replicas)
     for o in (2, 1, 3, 0):
         for j in (2, 1, 3, 0):
             if (o, j) != (0, 0):
                 send(piece, piece, send_sem.at[3], recv_sem.at[3], near_device(o, j))
-    wait(mates.at[0:7], recv_sem.at[2])
     wait(full.at[0 : 15 * PART], recv_sem.at[3])
 
     value = jnp.concatenate(split(full[rows(slab, CHUNK), :]), axis=1)
-    total = lax.dot_general(value, comb[rows(slab, CHUNK), :], (((0,), (0,)), ((), ())), preferred_element_type=F32)
-    for n in range(7):
-        total = total + lax.dot_general(value, mates[n], (((0,), (0,)), ((), ())), preferred_element_type=F32)
+    total = lax.dot_general(value, mate_sum[...], (((0,), (0,)), ((), ())), preferred_element_type=F32)
+    total = total[:, 0 : 2 * COLS] + total[:, 2 * COLS :]
     right[...] = (total[0:64, 0:COLS] + total[128:192, 0:COLS]) + (total[64:128, COLS:] + total[192:256, COLS:])
-    for n, (c, i) in enumerate(mate_offsets):
-        index, to = mate(c, i)
-        send(right.at[rows(index * 8, 8)], right_in.at[n], send_sem.at[4], recv_sem.at[4], to)
+    me, lot = core * 4 + y, rows((core * 4 + y) * 8, 8)
+    for o in (2, 1, 3, 0):
+        for c, i in mate_offsets + [(0, 0)]:
+            if (o, c, i) != (0, 0, 0):
+                to_core, to_y = core ^ c, (y + i) & 3
+                to = device(x, to_y, (z & 28) | near_at(o), to_core)
+                src = right.at[rows((to_core * 4 + to_y) * 8, 8)]
+                send(src, right_in.at[near * 8 + me], send_sem.at[4], recv_sem.at[4], to)
+    right_in[near * 8 + me] = right[lot, :]
     piece = full.at[rows(slab, CHUNK)]
     for i in (2, 1, 3):
         send(piece, piece, send_sem.at[5], recv_sem.at[5], device(x, (y + i) & 3, z, core))
-    lot = rows((core * 4 + y) * 8, 8)
-    wait(right_in, recv_sem.at[4])
-    total = right[lot, :]
-    for n in range(7):
-        total = total + right_in[n]
-    right_near_sum[0] = total
-    for o in (2, 1, 3):
-        send(right_near_sum.at[0], right_near.at[near], send_sem.at[6], recv_sem.at[6], near_device(o))
-    right_near[near] = right_near_sum[0]
-    wait(full.at[0 : 3 * CHUNK], recv_sem.at[5])
-    half = full.at[rows(own, OWN)]
-    send(half, half, core_send.at[4], core_recv.at[4], other)
 
     def gram_of(start):
         total = None
@@ -243,13 +242,19 @@
             total = term if total is None else total + term
         return total
 
-    wait(right_near.at[0:3], recv_sem.at[6])
-    right_near_sum[1] = ((right_near[0] + right_near[1]) + right_near[2]) + right_near[3]
+    wait(full.at[0 : 3 * CHUNK], recv_sem.at[5])
+    half = full.at[rows(own, OWN)]
+    send(half, half, core_send.at[4], core_recv.at[4], other)
+    grams[core] = gram_of(own)
+    wait(right_in.at[0:31], recv_sem.at[4])
+    total = right_in[0]
+    for n in range(1, 32):
+        total = total + right_in[n]
+    right_sum[...] = total
     line = far & 3
     for o in (2, 1, 3):
-        send(right_near_sum.at[1], right_far.at[line], send_sem.at[7], recv_sem.at[7], in_line(o))
-    right_far[line] = right_near_sum[1]
-    grams[core] = gram_of(own)
+        send(right_sum, right_far.at[line], send_sem.at[7], recv_sem.at[7], in_line(o))
+    right_far[line] = right_sum[...]
     wait(half, core_recv.at[4])
     grams[1 - core] = gram_of(theirs)
     gram = grams[0] + grams[1]
@@ -286,11 +291,10 @@
     wait(near_in.at[0:3], send_sem.at[1])
     wait(mates.at[0:7], send_sem.at[2])
     wait(full.at[0 : 15 * PART], send_sem.at[3])
-    wait(right_in, send_sem.at[4])
+    wait(right_in.at[0:31], send_sem.at[4])
     wait(full.at[0 : 3 * CHUNK], send_sem.at[5])
-    wait(right_near.at[0:3], send_sem.at[6])
-    wait(right_near.at[0:3], send_sem.at[7])
-    wait(right_in, send_sem.at[8])
+    wait(right_far.at[0:3], send_sem.at[7])
+    wait(right_in.at[0:7], send_sem.at[8])
     for n in range(7):
         wait(near_sum, far_send.at[n])
     comb_copy.wait()
@@ -334,9 +338,10 @@
             vmem((128, 2 * COLS), BF16), vmem((HALF, 128), F32), vmem((4, CHUNK, 128), F32),
             vmem((16, BLOCK, 128), F32), vmem((BLOCK, 128), F32), vmem((4, PART, 128), F32), vmem((PART, 128), F32),
             vmem((8, PART, 128), F32), vmem((HALF, 128), F32), vmem((7, CHUNK, 2 * COLS), BF16),
+            vmem((CHUNK, 4 * COLS), BF16),
             vmem((HALF, 256), BF16), vmem((2, 256, 256), F32), vmem((HALF, 128), BF16),
-            vmem((RANK, COLS), F32), vmem((7, 8, COLS), F32), vmem((4, 8, COLS), F32),
-            vmem((2, 8, COLS), F32), vmem((4, 8, COLS), F32), vmem((RANK, COLS), F32),
+            vmem((RANK, COLS), F32), vmem((32, 8, COLS), F32), vmem((8, COLS), F32),
+            vmem((4, 8, COLS), F32), vmem((RANK, COLS), F32),
             dma((4,)), dma((5,)), dma((5,)), dma((9,)), dma((9,)), dma((7,)), dma((7,)),
             pltpu.SemaphoreType.REGULAR((4,)),
         ],

time: 80.7 us -> 79.3 us (0.983)
  Pallas kernels: 79.1 us -> 77.7 us
    pallas_call x1, Pallas kernels: 77.4 us -> 76 us  [local(): pl.pallas_call(functools.partial(exchange_kernel, replicas), name='exchan...]
where the time goes in v4:
time: 79.3 us; the launch traced here: 79.1 us
  Pallas kernels  77.7 us (98%)
    pallas_call x1, Pallas kernels, local(): pl.pallas_call(functools.partial(exchange_kernel, replicas), name='exchan...  76 us
    pallas_call x1, Pallas kernels, local(): pl.pallas_call(finish_kernel, name='finish', out_shape=(jax.ShapeDtypeStr...  1.66 us

profile of v4, /device:TPU:1, one launch (start us, length us, event | category | flops | bytes accessed | tf_op | source)
XLA Modules:
  0.0 79.1 jit_solution(7543917617575235340)
XLA Ops:
  0.6 0.0 copy-start
  0.6 0.7 copy-done
  1.4 76.0 %exchange.1 = (bf16[2048,128]{1,0:T(8,128)(2,1)S(1)}, bf16[2048,256]{1,0:T(8,128)(2,1)S(1)}, f32[64,128]{1,0:T(8,128)S(1)}) custom-call(bf16[1,4096,128]{2,1,0:T(8,128)(2,1)} %grads.1, bf16[1,4096,128]{2,1,0:T(8,128)(2,1)} %errors.1, f32[64,128]{1,0:T(8,128)S(1)} %bitcast.4), custom_call_target="tpu_custom_call" | custom-call | tf_op jit(solution)/shard_map/exchange/pallas_call | solution.py:326
  77.4 1.7 %finish.1 = (bf16[2,2048,128]{2,1,0:T(8,128)(2,1)}, bf16[2,2048,128]{2,1,0:T(8,128)(2,1)}, f32[64,128]{1,0:T(8,128)}) custom-call(bf16[2048,128]{1,0:T(8,128)(2,1)S(1)} %get-tuple-element.9.q, bf16[2048,256]{1,0:T(8,128)(2,1)S(1)} %get-tuple-element.10.comb, f32[64,128]{1,0:T(8,128)S(1)} %get-tuple-element.11.right), custom_call_target="tpu_custom_call" | custom-call | tf_op jit(solution)/shard_map/finish/pallas_call | solution.py:350
Async XLA Ops:
  0.6 0.8 copy-start

commit v5 on v4

--- a/solution.py
+++ b/solution.py
@@ -74,7 +74,7 @@
 
 def exchange_kernel(
     replicas, grads, errors, basis, q_out, comb_out, right_out,
-    g_in, e_in, comb, blocks, part, from_core, plane_in, plane_sum, near_in, near_sum, far_in, full, mates, mate_sum, pieces, grams,
+    g_in, e_in, basis_in, comb, blocks, part, from_core, plane_in, plane_sum, near_in, near_sum, far_in, full, mates, mate_sum, pieces, grams,
     q, right, right_in, right_sum, right_far, right_full,
     local_sem, core_send, core_recv, send_sem, recv_sem, far_send, far_recv, tokens,
 ):
@@ -118,13 +118,15 @@
     line_x = [device(*plane(0, j), z, core) for j in (2, 1, 3)]
     line_y = [device(*plane(i, 0), z, core) for i in (2, 1, 3)]
     signal(barrier, line_x + line_y + [along(1), along(31), other])
+    pltpu.make_async_copy(basis, basis_in, local_sem.at[4]).start()
     for n, start in enumerate((theirs, own)):
         for base in (0, HALF):
             here = rows(base + start, OWN)
             pltpu.make_async_copy(grads.at[0, here], g_in.at[here], local_sem.at[n]).start()
             pltpu.make_async_copy(errors.at[0, here], e_in.at[here], local_sem.at[n]).start()
 
-    blocks[...] = twice(basis[...].astype(BF16))
+    wait(basis_in, local_sem.at[4])
+    blocks[...] = twice(basis_in[...].astype(BF16))
     lanes = lax.broadcasted_iota(jnp.int32, (RANK, 128), 1)
     at = lax.broadcasted_iota(jnp.int32, (RANK, 128), 0)
 
@@ -331,10 +333,10 @@
             jax.ShapeDtypeStruct((HALF, 2 * COLS), BF16),
             jax.ShapeDtypeStruct((RANK, COLS), F32),
         ),
-        in_specs=[anywhere] * 2 + [inside],
+        in_specs=[pl.BlockSpec(memory_space=pltpu.HBM)] * 3,
         out_specs=(anywhere, anywhere, inside),
         scratch_shapes=[
-            vmem((2 * HALF, COLS), BF16), vmem((2 * HALF, COLS), BF16), vmem((HALF, 2 * COLS), BF16),
+            vmem((2 * HALF, COLS), BF16), vmem((2 * HALF, COLS), BF16), vmem((RANK, COLS), F32), vmem((HALF, 2 * COLS), BF16),
             vmem((128, 2 * COLS), BF16), vmem((HALF, 128), F32), vmem((4, CHUNK, 128), F32),
             vmem((16, BLOCK, 128), F32), vmem((BLOCK, 128), F32), vmem((4, PART, 128), F32), vmem((PART, 128), F32),
             vmem((8, PART, 128), F32), vmem((HALF, 128), F32), vmem((7, CHUNK, 2 * COLS), BF16),
@@ -342,11 +344,11 @@
             vmem((HALF, 256), BF16), vmem((2, 256, 256), F32), vmem((HALF, 128), BF16),
             vmem((RANK, COLS), F32), vmem((32, 8, COLS), F32), vmem((8, COLS), F32),
             vmem((4, 8, COLS), F32), vmem((RANK, COLS), F32),
-            dma((4,)), dma((5,)), dma((5,)), dma((9,)), dma((9,)), dma((7,)), dma((7,)),
+            dma((5,)), dma((5,)), dma((5,)), dma((9,)), dma((9,)), dma((7,)), dma((7,)),
             pltpu.SemaphoreType.REGULAR((4,)),
         ],
         compiler_params=pltpu.CompilerParams(collective_id=0, has_side_effects=True, vmem_limit_bytes=52 << 20),
-    )(grads, errors, basis.T)
+    )(grads, errors, pltpu.with_memory_space_constraint(basis.T, pltpu.HBM))
     approx, new_errors, new_basis = pl.pallas_call(
         finish_kernel,
         name="finish",

time: 79.3 us -> 78.6 us (level)
  no operation moved by 1% of the time
where the time goes in v5:
time: 78.6 us; the launch traced here: 78.4 us
  Pallas kernels  77.8 us (99%)
    pallas_call x1, Pallas kernels, local(): pl.pallas_call(functools.partial(exchange_kernel, replicas), name='exchan...  76.1 us
    pallas_call x1, Pallas kernels, local(): pl.pallas_call(finish_kernel, name='finish', out_shape=(jax.ShapeDtypeStr...  1.67 us

profile of v5, /device:TPU:1, one launch (start us, length us, event | category | flops | bytes accessed | tf_op | source)
XLA Modules:
  0.0 78.4 jit_solution(4215824089097360708)
XLA Ops:
  0.6 76.1 %exchange.1 = (bf16[2048,128]{1,0:T(8,128)(2,1)S(1)}, bf16[2048,256]{1,0:T(8,128)(2,1)S(1)}, f32[64,128]{1,0:T(8,128)S(1)}) custom-call(bf16[1,4096,128]{2,1,0:T(8,128)(2,1)} %grads.1, bf16[1,4096,128]{2,1,0:T(8,128)(2,1)} %errors.1, f32[64,128]{1,0:T(8,128)} %bitcast.4), custom_call_target="tpu_custom_call" | custom-call | tf_op jit(solution)/shard_map/exchange/pallas_call | solution.py:328
  76.8 1.7 %finish.1 = (bf16[2,2048,128]{2,1,0:T(8,128)(2,1)}, bf16[2,2048,128]{2,1,0:T(8,128)(2,1)}, f32[64,128]{1,0:T(8,128)}) custom-call(bf16[2048,128]{1,0:T(8,128)(2,1)S(1)} %get-tuple-element.9.q, bf16[2048,256]{1,0:T(8,128)(2,1)S(1)} %get-tuple-element.10.comb, f32[64,128]{1,0:T(8,128)S(1)} %get-tuple-element.11.right), custom_call_target="tpu_custom_call" | custom-call | tf_op jit(solution)/shard_map/finish/pallas_call | solution.py:352

commit v6 on v5

--- a/solution.py
+++ b/solution.py
@@ -166,8 +166,6 @@
             pl.semaphore_wait(tokens.at[0], 3)
             pl.semaphore_wait(tokens.at[1], 2)
             signal(tokens.at[2], [along(2), along(30)])
-    comb_copy = pltpu.make_async_copy(comb, comb_out, local_sem.at[2])
-    comb_copy.start()
     plane_in[mine] = part[rows(own + mine * BLOCK, BLOCK), :]
     pl.semaphore_wait(tokens.at[2], 2)
     signal(tokens.at[3], [along(4), along(28)])
@@ -257,6 +255,8 @@
     for o in (2, 1, 3):
         send(right_sum, right_far.at[line], send_sem.at[7], recv_sem.at[7], in_line(o))
     right_far[line] = right_sum[...]
+    comb_copy = pltpu.make_async_copy(comb, comb_out, local_sem.at[2])
+    comb_copy.start()
     wait(half, core_recv.at[4])
     grams[1 - core] = gram_of(theirs)
     gram = grams[0] + grams[1]

time: 78.6 us -> 78.6 us (level)
  no operation moved by 1% of the time
where the time goes in v6:
time: 78.6 us; the launch traced here: 78.4 us
  Pallas kernels  77.8 us (99%)
    pallas_call x1, Pallas kernels, local(): pl.pallas_call(functools.partial(exchange_kernel, replicas), name='exchan...  76.1 us
    pallas_call x1, Pallas kernels, local(): pl.pallas_call(finish_kernel, name='finish', out_shape=(jax.ShapeDtypeStr...  1.66 us

profile of v6, /device:TPU:1, one launch (start us, length us, event | category | flops | bytes accessed | tf_op | source)
XLA Modules:
  0.0 78.4 jit_solution(7758728692949369130)
XLA Ops:
  0.6 76.1 %exchange.1 = (bf16[2048,128]{1,0:T(8,128)(2,1)S(1)}, bf16[2048,256]{1,0:T(8,128)(2,1)S(1)}, f32[64,128]{1,0:T(8,128)S(1)}) custom-call(bf16[1,4096,128]{2,1,0:T(8,128)(2,1)} %grads.1, bf16[1,4096,128]{2,1,0:T(8,128)(2,1)} %errors.1, f32[64,128]{1,0:T(8,128)} %bitcast.4), custom_call_target="tpu_custom_call" | custom-call | tf_op jit(solution)/shard_map/exchange/pallas_call | solution.py:328
  76.8 1.7 %finish.1 = (bf16[2,2048,128]{2,1,0:T(8,128)(2,1)}, bf16[2,2048,128]{2,1,0:T(8,128)(2,1)}, f32[64,128]{1,0:T(8,128)}) custom-call(bf16[2048,128]{1,0:T(8,128)(2,1)S(1)} %get-tuple-element.9.q, bf16[2048,256]{1,0:T(8,128)(2,1)S(1)} %get-tuple-element.10.comb, f32[64,128]{1,0:T(8,128)S(1)} %get-tuple-element.11.right), custom_call_target="tpu_custom_call" | custom-call | tf_op jit(solution)/shard_map/finish/pallas_call | solution.py:352
